TPU v7x, 32 devices: a whole 2x2x4 slice. The times are simulated.
32 devices in a mesh: dp: 8 (over z, y), mem: 4 (over x, core).
Axes of the slice: x: 2, y: 2, z: 4, core: 2. Of those that a mesh axis runs over, the one named last changes fastest.
Arguments:
- target: bfloat16 [128, 256, 512], P(('dp', 'mem')), may hold values from -6 to 6
- memory: bfloat16 [128, 256, 512], P('dp', 'mem'), may hold values from -6 to 6
- time_steps: int32 [128], P(('dp', 'mem')), may hold values from 0 to 49
- target_len: int32 [128], P(('dp', 'mem')), may hold values from 1 to 256, 20480 in all
- source_len: int32 [128], P('dp'), may hold values from 64 to 256, as said below
- source_off: int32 [128], P('dp'), may hold values from 0 to 192, as said below
- cotangent: bfloat16 [128, 256, 512], P(('dp', 'mem')), may hold values from -6 to 6
- self_query: bfloat16 [512, 512], P('dp', 'mem'), may hold values from -0.25 to 0.25
- self_key: bfloat16 [512, 512], P('dp', 'mem'), may hold values from -0.25 to 0.25
- self_value: bfloat16 [512, 512], P('dp', 'mem'), may hold values from -0.25 to 0.25
- self_out: bfloat16 [512, 512], P('dp', 'mem'), may hold values from -1.5 to 1.5
- cross_query: bfloat16 [512, 512], P('dp', 'mem'), may hold values from -0.25 to 0.25
- cross_key: bfloat16 [512, 512], P('dp', 'mem'), may hold values from -0.25 to 0.25
- cross_value: bfloat16 [512, 512], P('dp', 'mem'), may hold values from -0.25 to 0.25
- cross_out: bfloat16 [512, 512], P('dp', 'mem'), may hold values from -1.5 to 1.5
- feed_in: bfloat16 [512, 2048], P('dp', 'mem'), may hold values from -0.25 to 0.25
- feed_out: bfloat16 [2048, 512], P('dp', 'mem'), may hold values from -0.125 to 0.125
- biases: bfloat16 [7, 512], P(None, 'dp'), may hold values from -4 to 4
- feed_bias: bfloat16 [2048], P('dp'), may hold values from -4 to 4
- norm_gain: bfloat16 [3, 512], P(None, 'dp'), may hold values from 0.5 to 1.5
- norm_shift: bfloat16 [3, 512], P(None, 'dp'), may hold values from -4 to 4
- step_table: bfloat16 [50, 512], P(None, 'dp'), may hold values from -6 to 6
Outputs:
- layer_out: bfloat16 [128, 256, 512], P(('dp', 'mem'))
- grad_target: float32 [128, 256, 512], P(('dp', 'mem'))
- grad_memory: float32 [128, 256, 512], P('dp', 'mem')
- grad_self_query: float32 [512, 512], P('dp', 'mem')
- grad_self_key: float32 [512, 512], P('dp', 'mem')
- grad_self_value: float32 [512, 512], P('dp', 'mem')
- grad_self_out: float32 [512, 512], P('dp', 'mem')
- grad_cross_query: float32 [512, 512], P('dp', 'mem')
- grad_cross_key: float32 [512, 512], P('dp', 'mem')
- grad_cross_value: float32 [512, 512], P('dp', 'mem')
- grad_cross_out: float32 [512, 512], P('dp', 'mem')
- grad_feed_in: float32 [512, 2048], P('dp', 'mem')
- grad_feed_out: float32 [2048, 512], P('dp', 'mem')
- grad_biases: float32 [7, 512], P(None, 'dp')
- grad_feed_bias: float32 [2048], P('dp')
- grad_norm_gain: float32 [3, 512], P(None, 'dp')
- grad_norm_shift: float32 [3, 512], P(None, 'dp')
- grad_step_table: float32 [50, 512], P(None, 'dp')
Inputs may be any that keep to these rules, and one draw needn't show every extreme that they name: `target_len`: some target has exactly 256 tokens. `source_len`: among the 16 pairs of each index of dp, one source has exactly 256 tokens and another exactly 64. A source occupies memory positions source_off to source_off + source_len - 1, so source_off + source_len is at most 256.
All inputs are finite; a program needn't handle non-finite values. No bound on the sum of `target_len` on one device may be relied on, other than what follows from the above.
Results may differ from a plain program's by a relative error of at most 0.025.
Values may be sent and summed in bfloat16 or wider, within the bound.
No kernel may reach another device: no remote copies, remote signals or barrier semaphores. Data moves between devices by JAX's collectives and lax.ppermute only.
A program may use at most 192 MiB of HBM per device.

v0:
```python
from functools import partial
import math

import jax
import jax.numpy as jnp
from jax import lax
from jax.sharding import PartitionSpec as P

HEADS = 8
DH = 64


norm_epsilon = 1e-05


def joined(shard, axis, join):
    gathered = jax.tree.map(
        lambda a, kind: lax.all_gather(a.astype(kind), axis),
        shard,
        (jnp.bfloat16, jnp.bfloat16, jnp.bfloat16),
    )

    def take(source):
        return jax.tree.map(
            lambda a, own: lax.dynamic_index_in_dim(a, source, 0, False).astype(own.dtype),
            gathered,
            shard,
        )

    return lax.fori_loop(
        1, lax.axis_size(axis), lambda source, state: join(state, take(source)), take(0)
    )


def product(left, right):
    return jnp.dot(left, right, preferred_element_type=jnp.float32)


def back_product(left, right):
    return lax.dot_general(
        left, right, (((left.ndim - 1,), (1,)), ((), ())), preferred_element_type=jnp.float32
    )


def outer_sum(left, right):
    left_flat = left.reshape(-1, left.shape[-1])
    right_flat = right.reshape(-1, right.shape[-1])
    return lax.dot_general(
        left_flat, right_flat, (((0,), (0,)), ((), ())), preferred_element_type=jnp.float32
    )


def norm_parts(signal, gain_vec, shift_vec):
    centre = signal - jnp.mean(signal, axis=-1, keepdims=True)
    inverse = lax.rsqrt(jnp.mean(centre * centre, axis=-1, keepdims=True) + norm_epsilon)
    scaled = centre * inverse
    return (scaled * gain_vec + shift_vec, scaled, inverse)


def norm_back(grad_norm, scaled, inverse, gain_vec):
    grad_scaled = grad_norm * gain_vec
    grad_signal = inverse * (
        grad_scaled
        - jnp.mean(grad_scaled, axis=-1, keepdims=True)
        - scaled * jnp.mean(grad_scaled * scaled, axis=-1, keepdims=True)
    )
    return (grad_signal, jnp.sum(grad_norm * scaled, axis=(0, 1)), jnp.sum(grad_norm, axis=(0, 1)))


def split_heads(signal):
    return signal.reshape(signal.shape[0], signal.shape[1], HEADS, DH)


def rescale(mixture, factor):
    return (split_heads(mixture) * jnp.swapaxes(factor, 1, 2)[..., None]).reshape(mixture.shape)


def score_block(queries, key_rows, allowed):
    scores = jnp.einsum(
        "bqhd,bkhd->bhqk",
        split_heads(queries),
        split_heads(key_rows),
        preferred_element_type=jnp.float32,
    ) * (1.0 / math.sqrt(DH))
    return jnp.where(allowed[:, None, None, :], scores, -1e30)


def attend(queries, key_rows, value_rows, allowed):
    scores = score_block(queries, key_rows, allowed)
    top_score = jnp.max(scores, axis=-1, keepdims=True)
    raised = jnp.exp(scores - top_score)
    total = jnp.sum(raised, axis=-1, keepdims=True)
    weights = (raised / total).astype(jnp.bfloat16)
    mixture = jnp.einsum(
        "bhqk,bkhd->bqhd", weights, split_heads(value_rows), preferred_element_type=jnp.float32
    )
    return (mixture.reshape(queries.shape), (top_score + jnp.log(total))[..., 0])


def partial_attend(queries, key_rows, value_rows, allowed):
    scores = score_block(queries, key_rows, allowed)
    top_score = jnp.max(scores, axis=-1)
    raised = jnp.where(allowed[:, None, None, :], jnp.exp(scores - top_score[..., None]), 0.0)
    total = jnp.sum(raised, axis=-1)
    mixture = jnp.einsum(
        "bhqk,bkhd->bqhd",
        raised.astype(jnp.bfloat16),
        split_heads(value_rows),
        preferred_element_type=jnp.float32,
    )
    return (top_score, total, mixture.reshape(queries.shape))


def combine_parts(earlier, later):
    top_one, total_one, mix_one = earlier
    top_two, total_two, mix_two = later
    top_score = jnp.maximum(top_one, top_two)
    factor_one = jnp.exp(top_one - top_score)
    factor_two = jnp.exp(top_two - top_score)
    return (
        top_score,
        total_one * factor_one + total_two * factor_two,
        rescale(mix_one, factor_one) + rescale(mix_two, factor_two),
    )


def attention_grads(grad_scores, weights, queries, key_rows, grad_heads):
    rounded = grad_scores.astype(jnp.bfloat16)
    factor = 1.0 / math.sqrt(DH)
    grad_query = (
        jnp.einsum(
            "bhqk,bkhd->bqhd", rounded, split_heads(key_rows), preferred_element_type=jnp.float32
        )
        * factor
    )
    grad_key = (
        jnp.einsum(
            "bhqk,bqhd->bkhd", rounded, split_heads(queries), preferred_element_type=jnp.float32
        )
        * factor
    )
    grad_value = jnp.einsum(
        "bhqk,bqhd->bkhd",
        weights.astype(jnp.bfloat16),
        grad_heads,
        preferred_element_type=jnp.float32,
    )
    return (
        grad_query.reshape(queries.shape),
        grad_key.reshape(key_rows.shape),
        grad_value.reshape(key_rows.shape),
    )


def attend_back(queries, key_rows, value_rows, allowed, log_total, grad_mix):
    scores = score_block(queries, key_rows, allowed)
    weights = jnp.exp(scores - log_total[..., None])
    grad_heads = split_heads(grad_mix)
    grad_weights = jnp.einsum(
        "bqhd,bkhd->bhqk", grad_heads, split_heads(value_rows), preferred_element_type=jnp.float32
    )
    grad_scores = weights * (grad_weights - jnp.sum(grad_weights * weights, axis=-1, keepdims=True))
    return attention_grads(grad_scores, weights, queries, key_rows, grad_heads)


def shards(
    target,
    memory,
    time_steps,
    target_len,
    source_len,
    source_off,
    cotangent,
    self_query,
    self_key,
    self_value,
    self_out,
    cross_query,
    cross_key,
    cross_value,
    cross_out,
    feed_in,
    feed_out,
    biases,
    feed_bias,
    norm_gain,
    norm_shift,
    step_table,
):
    mem_index = lax.axis_index("mem")
    pairs = target.shape[0]
    length = target.shape[1]
    slice_len = memory.shape[1]
    wide = (
        lax.all_gather(self_query, "mem", axis=1, tiled=True),
        lax.all_gather(self_key, "mem", axis=1, tiled=True),
        lax.all_gather(self_value, "mem", axis=1, tiled=True),
        lax.all_gather(self_out, "mem", axis=1, tiled=True),
        lax.all_gather(cross_query, "mem", axis=1, tiled=True),
        lax.all_gather(cross_key, "mem", axis=1, tiled=True),
        lax.all_gather(cross_value, "mem", axis=1, tiled=True),
        lax.all_gather(cross_out, "mem", axis=1, tiled=True),
        lax.all_gather(feed_in, "mem", axis=1, tiled=True),
        lax.all_gather(feed_out, "mem", axis=1, tiled=True),
    )
    full_set = (
        lax.all_gather(wide[0], "dp", axis=0, tiled=True),
        lax.all_gather(wide[1], "dp", axis=0, tiled=True),
        lax.all_gather(wide[2], "dp", axis=0, tiled=True),
        lax.all_gather(wide[3], "dp", axis=0, tiled=True),
        lax.all_gather(wide[4], "dp", axis=0, tiled=True),
        lax.all_gather(wide[5], "dp", axis=0, tiled=True),
        lax.all_gather(wide[6], "dp", axis=0, tiled=True),
        lax.all_gather(wide[7], "dp", axis=0, tiled=True),
        lax.all_gather(wide[8], "dp", axis=0, tiled=True),
        lax.all_gather(wide[9], "dp", axis=0, tiled=True),
        lax.all_gather(biases, "dp", axis=1, tiled=True),
        lax.all_gather(feed_bias, "dp", axis=0, tiled=True),
        lax.all_gather(norm_gain, "dp", axis=1, tiled=True),
        lax.all_gather(norm_shift, "dp", axis=1, tiled=True),
        lax.all_gather(step_table, "dp", axis=1, tiled=True),
    )
    (
        query_self,
        key_self,
        value_self,
        out_self,
        query_cross,
        key_cross,
        value_cross,
        out_cross,
        expand_weight,
        reduce_weight,
        bias_rows,
        expand_bias,
        gain_rows,
        shift_rows,
        table_rows,
    ) = full_set
    step_hot = time_steps[:, None] == jnp.arange(table_rows.shape[0])[None, :]
    embedded = (
        target.astype(jnp.float32) + product(step_hot.astype(jnp.bfloat16), table_rows)[:, None, :]
    )
    normed_a, scaled_a, inverse_a = norm_parts(embedded, gain_rows[0], shift_rows[0])
    input_a = normed_a.astype(jnp.bfloat16)
    queries = (product(input_a, query_self) + bias_rows[0]).astype(jnp.bfloat16)
    key_rows = product(input_a, key_self).astype(jnp.bfloat16)
    value_rows = (product(input_a, value_self) + bias_rows[1]).astype(jnp.bfloat16)
    self_allowed = jnp.arange(length)[None, :] < target_len[:, None]
    mixed_self, log_self = attend(queries, key_rows, value_rows, self_allowed)
    mixed_self = mixed_self.astype(jnp.bfloat16)
    after_self = embedded + product(mixed_self, out_self) + bias_rows[2]
    normed_b, scaled_b, inverse_b = norm_parts(after_self, gain_rows[1], shift_rows[1])
    input_b = normed_b.astype(jnp.bfloat16)
    cross_rows = (product(input_b, query_cross) + bias_rows[3]).astype(jnp.bfloat16)
    memory_keys = product(memory, key_cross).astype(jnp.bfloat16)
    memory_values = (product(memory, value_cross) + bias_rows[4]).astype(jnp.bfloat16)
    every_query = lax.all_gather(cross_rows, "mem", axis=0, tiled=True)
    source_pos = mem_index * slice_len + jnp.arange(slice_len)[None, :]
    cross_allowed = (source_pos >= source_off[:, None]) & (
        source_pos < (source_off + source_len)[:, None]
    )
    top_part, total_part, mix_part = partial_attend(
        every_query, memory_keys, memory_values, cross_allowed
    )
    top_all, total_all, mix_all = joined((top_part, total_part, mix_part), "mem", combine_parts)
    merged_all = rescale(mix_all, 1.0 / total_all)
    log_cross = top_all + jnp.log(total_all)
    mixed_cross = lax.dynamic_slice_in_dim(merged_all, mem_index * pairs, pairs, 0)
    mixed_cross = mixed_cross.astype(jnp.bfloat16)
    after_cross = after_self + product(mixed_cross, out_cross) + bias_rows[5]
    normed_c, scaled_c, inverse_c = norm_parts(after_cross, gain_rows[2], shift_rows[2])
    input_c = normed_c.astype(jnp.bfloat16)
    hidden_pre = product(input_c, expand_weight) + expand_bias
    hidden_act = jax.nn.gelu(hidden_pre, approximate=False).astype(jnp.bfloat16)
    layer_out = after_cross + product(hidden_act, reduce_weight) + bias_rows[6]
    wide_back = (
        lax.all_gather(self_query, "mem", axis=1, tiled=True),
        lax.all_gather(self_key, "mem", axis=1, tiled=True),
        lax.all_gather(self_value, "mem", axis=1, tiled=True),
        lax.all_gather(self_out, "mem", axis=1, tiled=True),
        lax.all_gather(cross_query, "mem", axis=1, tiled=True),
        lax.all_gather(cross_key, "mem", axis=1, tiled=True),
        lax.all_gather(cross_value, "mem", axis=1, tiled=True),
        lax.all_gather(cross_out, "mem", axis=1, tiled=True),
        lax.all_gather(feed_in, "mem", axis=1, tiled=True),
        lax.all_gather(feed_out, "mem", axis=1, tiled=True),
    )
    back_set = (
        lax.all_gather(wide_back[0], "dp", axis=0, tiled=True),
        lax.all_gather(wide_back[1], "dp", axis=0, tiled=True),
        lax.all_gather(wide_back[2], "dp", axis=0, tiled=True),
        lax.all_gather(wide_back[3], "dp", axis=0, tiled=True),
        lax.all_gather(wide_back[4], "dp", axis=0, tiled=True),
        lax.all_gather(wide_back[5], "dp", axis=0, tiled=True),
        lax.all_gather(wide_back[6], "dp", axis=0, tiled=True),
        lax.all_gather(wide_back[7], "dp", axis=0, tiled=True),
        lax.all_gather(wide_back[8], "dp", axis=0, tiled=True),
        lax.all_gather(wide_back[9], "dp", axis=0, tiled=True),
        lax.all_gather(biases, "dp", axis=1, tiled=True),
        lax.all_gather(feed_bias, "dp", axis=0, tiled=True),
        lax.all_gather(norm_gain, "dp", axis=1, tiled=True),
        lax.all_gather(norm_shift, "dp", axis=1, tiled=True),
        lax.all_gather(step_table, "dp", axis=1, tiled=True),
    )
    (
        query_self,
        key_self,
        value_self,
        out_self,
        query_cross,
        key_cross,
        value_cross,
        out_cross,
        expand_weight,
        reduce_weight,
        bias_rows,
        expand_bias,
        gain_rows,
        shift_rows,
        table_rows,
    ) = back_set
    grad_out = cotangent.astype(jnp.float32)
    grad_bias_six = jnp.sum(grad_out, axis=(0, 1))
    grad_reduce = outer_sum(hidden_act, cotangent)
    grad_act = back_product(cotangent, reduce_weight)
    hidden_again = product(input_c, expand_weight) + expand_bias
    unused_value, gelu_pull = jax.vjp(partial(jax.nn.gelu, approximate=False), hidden_again)
    grad_pre = gelu_pull(grad_act)[0].astype(jnp.bfloat16)
    grad_expand_bias = jnp.sum(grad_pre.astype(jnp.float32), axis=(0, 1))
    grad_expand = outer_sum(input_c, grad_pre)
    grad_in_c, gain_grad_c, shift_grad_c = norm_back(
        back_product(grad_pre, expand_weight), scaled_c, inverse_c, gain_rows[2]
    )
    grad_cross_res = grad_out + grad_in_c
    grad_branch_b = grad_cross_res.astype(jnp.bfloat16)
    grad_bias_five = jnp.sum(grad_branch_b.astype(jnp.float32), axis=(0, 1))
    grad_out_cross = outer_sum(mixed_cross, grad_branch_b)
    grad_mixed_b = back_product(grad_branch_b, out_cross).astype(jnp.bfloat16)
    every_grad = lax.all_gather(grad_mixed_b, "mem", axis=0, tiled=True)
    scores = score_block(every_query, memory_keys, cross_allowed)
    weights = jnp.exp(scores - log_cross[..., None])
    grad_heads = split_heads(every_grad)
    offset = jnp.swapaxes(
        jnp.sum(split_heads(merged_all) * grad_heads.astype(jnp.float32), axis=-1), 1, 2
    )
    grad_weights = jnp.einsum(
        "bqhd,bkhd->bhqk",
        grad_heads,
        split_heads(memory_values),
        preferred_element_type=jnp.float32,
    )
    grad_scores = weights * (grad_weights - offset[..., None])
    query_part, key_local, value_local = attention_grads(
        grad_scores, weights, every_query, memory_keys, grad_heads
    )
    grad_cross_q = lax.psum_scatter(
        query_part.astype(jnp.bfloat16), "mem", scatter_dimension=0, tiled=True
    )
    grad_keys = key_local.astype(jnp.bfloat16)
    grad_values = value_local.astype(jnp.bfloat16)
    grad_bias_three = jnp.sum(grad_cross_q.astype(jnp.float32), axis=(0, 1))
    grad_query_cross = outer_sum(input_b, grad_cross_q)
    grad_key_cross = outer_sum(memory, grad_keys)
    grad_value_cross = outer_sum(memory, grad_values)
    grad_bias_four = jnp.sum(grad_values.astype(jnp.float32), axis=(0, 1))
    grad_memory = back_product(grad_keys, key_cross) + back_product(grad_values, value_cross)
    grad_in_b, gain_grad_b, shift_grad_b = norm_back(
        back_product(grad_cross_q, query_cross), scaled_b, inverse_b, gain_rows[1]
    )
    grad_self_res = grad_cross_res + grad_in_b
    grad_branch_a = grad_self_res.astype(jnp.bfloat16)
    grad_bias_two = jnp.sum(grad_branch_a.astype(jnp.float32), axis=(0, 1))
    grad_out_self = outer_sum(mixed_self, grad_branch_a)
    grad_mixed_a = back_product(grad_branch_a, out_self).astype(jnp.bfloat16)
    self_q_grad, self_k_grad, self_v_grad = attend_back(
        queries, key_rows, value_rows, self_allowed, log_self, grad_mixed_a
    )
    self_q_grad = self_q_grad.astype(jnp.bfloat16)
    self_k_grad = self_k_grad.astype(jnp.bfloat16)
    self_v_grad = self_v_grad.astype(jnp.bfloat16)
    grad_bias_zero = jnp.sum(self_q_grad.astype(jnp.float32), axis=(0, 1))
    grad_bias_one = jnp.sum(self_v_grad.astype(jnp.float32), axis=(0, 1))
    grad_query_self = outer_sum(input_a, self_q_grad)
    grad_key_self = outer_sum(input_a, self_k_grad)
    grad_value_self = outer_sum(input_a, self_v_grad)
    grad_normed_a = (
        back_product(self_q_grad, query_self)
        + back_product(self_k_grad, key_self)
        + back_product(self_v_grad, value_self)
    )
    grad_in_a, gain_grad_a, shift_grad_a = norm_back(
        grad_normed_a, scaled_a, inverse_a, gain_rows[0]
    )
    grad_target = grad_self_res + grad_in_a
    grad_table = lax.dot_general(
        step_hot.astype(jnp.float32),
        jnp.sum(grad_target, axis=1),
        (((0,), (0,)), ((), ())),
        precision=lax.Precision.HIGHEST,
        preferred_element_type=jnp.float32,
    )
    grad_bias_rows = jnp.stack(
        [
            grad_bias_zero,
            grad_bias_one,
            grad_bias_two,
            grad_bias_three,
            grad_bias_four,
            grad_bias_five,
            grad_bias_six,
        ]
    )
    grad_gain_rows = jnp.stack([gain_grad_a, gain_grad_b, gain_grad_c])
    grad_shift_rows = jnp.stack([shift_grad_a, shift_grad_b, shift_grad_c])
    reduced = (
        lax.psum_scatter(grad_query_self, "dp", scatter_dimension=0, tiled=True),
        lax.psum_scatter(grad_key_self, "dp", scatter_dimension=0, tiled=True),
        lax.psum_scatter(grad_value_self, "dp", scatter_dimension=0, tiled=True),
        lax.psum_scatter(grad_out_self, "dp", scatter_dimension=0, tiled=True),
        lax.psum_scatter(grad_query_cross, "dp", scatter_dimension=0, tiled=True),
        lax.psum_scatter(grad_key_cross, "dp", scatter_dimension=0, tiled=True),
        lax.psum_scatter(grad_value_cross, "dp", scatter_dimension=0, tiled=True),
        lax.psum_scatter(grad_out_cross, "dp", scatter_dimension=0, tiled=True),
        lax.psum_scatter(grad_expand, "dp", scatter_dimension=0, tiled=True),
        lax.psum_scatter(grad_reduce, "dp", scatter_dimension=0, tiled=True),
        lax.psum_scatter(grad_bias_rows, "dp", scatter_dimension=1, tiled=True),
        lax.psum_scatter(grad_expand_bias, "dp", scatter_dimension=0, tiled=True),
        lax.psum_scatter(grad_gain_rows, "dp", scatter_dimension=1, tiled=True),
        lax.psum_scatter(grad_shift_rows, "dp", scatter_dimension=1, tiled=True),
        lax.psum_scatter(grad_table, "dp", scatter_dimension=1, tiled=True),
    )
    narrow = (
        lax.psum_scatter(
            reduced[0].astype(jnp.bfloat16), "mem", scatter_dimension=1, tiled=True
        ).astype(jnp.float32),
        lax.psum_scatter(
            reduced[1].astype(jnp.bfloat16), "mem", scatter_dimension=1, tiled=True
        ).astype(jnp.float32),
        lax.psum_scatter(
            reduced[2].astype(jnp.bfloat16), "mem", scatter_dimension=1, tiled=True
        ).astype(jnp.float32),
        lax.psum_scatter(
            reduced[3].astype(jnp.bfloat16), "mem", scatter_dimension=1, tiled=True
        ).astype(jnp.float32),
        lax.psum_scatter(
            reduced[4].astype(jnp.bfloat16), "mem", scatter_dimension=1, tiled=True
        ).astype(jnp.float32),
        lax.psum_scatter(
            reduced[5].astype(jnp.bfloat16), "mem", scatter_dimension=1, tiled=True
        ).astype(jnp.float32),
        lax.psum_scatter(
            reduced[6].astype(jnp.bfloat16), "mem", scatter_dimension=1, tiled=True
        ).astype(jnp.float32),
        lax.psum_scatter(
            reduced[7].astype(jnp.bfloat16), "mem", scatter_dimension=1, tiled=True
        ).astype(jnp.float32),
        lax.psum_scatter(
            reduced[8].astype(jnp.bfloat16), "mem", scatter_dimension=1, tiled=True
        ).astype(jnp.float32),
        lax.psum_scatter(
            reduced[9].astype(jnp.bfloat16), "mem", scatter_dimension=1, tiled=True
        ).astype(jnp.float32),
    )
    small_set = lax.psum((reduced[10], reduced[11], reduced[12], reduced[13], reduced[14]), "mem")
    return (
        layer_out.astype(jnp.bfloat16),
        grad_target,
        grad_memory,
        narrow[0],
        narrow[1],
        narrow[2],
        narrow[3],
        narrow[4],
        narrow[5],
        narrow[6],
        narrow[7],
        narrow[8],
        narrow[9],
        small_set[0],
        small_set[1],
        small_set[2],
        small_set[3],
        small_set[4],
    )


def solution(mesh):
    return jax.shard_map(
        shards,
        mesh=mesh,
        in_specs=(
            P(("dp", "mem"), None, None),
            P("dp", "mem", None),
            P(("dp", "mem")),
            P(("dp", "mem")),
            P("dp"),
            P("dp"),
            P(("dp", "mem"), None, None),
            P("dp", "mem"),
            P("dp", "mem"),
            P("dp", "mem"),
            P("dp", "mem"),
            P("dp", "mem"),
            P("dp", "mem"),
            P("dp", "mem"),
            P("dp", "mem"),
            P("dp", "mem"),
            P("dp", "mem"),
            P(None, "dp"),
            P("dp"),
            P(None, "dp"),
            P(None, "dp"),
            P(None, "dp"),
        ),
        out_specs=(
            P(("dp", "mem"), None, None),
            P(("dp", "mem"), None, None),
            P("dp", "mem", None),
            P("dp", "mem"),
            P("dp", "mem"),
            P("dp", "mem"),
            P("dp", "mem"),
            P("dp", "mem"),
            P("dp", "mem"),
            P("dp", "mem"),
            P("dp", "mem"),
            P("dp", "mem"),
            P("dp", "mem"),
            P(None, "dp"),
            P("dp"),
            P(None, "dp"),
            P(None, "dp"),
            P(None, "dp"),
        ),
        check_vma=False,
    )
```

profile of v0, /device:TPU:0, one launch (start us, length us, event | category | flops | bytes accessed | tf_op | source)
XLA Modules:
  0.0 1978.1 jit_solution(2357881916609775897)
XLA Ops:
  7.3 32.7 %all-gather.2 = bf16[8,64,50]{1,2,0:T(8,128)(2,1)S(1)} all-gather(bf16[1,64,50]{1,2,0:T(8,128)(2,1)} %bitcast.352), channel_id=1, replica_groups=mesh['dp'=8,'mem'=4] {'dp'}, dimensions={0}, use_global_device_ids=true | all-gather | bytes 57600 | tf_op jit(solution)/shard_map/all_gather | solution.py:221
  44.2 20.7 %all-gather.3 = bf16[8,64,3]{1,2,0:T(4,128)(2,1)S(1)} all-gather(bf16[1,64,3]{1,2,0:T(4,128)(2,1)} %bitcast.391), channel_id=1, replica_groups=mesh['dp'=8,'mem'=4] {'dp'}, dimensions={0}, use_global_device_ids=true | all-gather | bytes 3456 | tf_op jit(solution)/shard_map/all_gather | solution.py:219
  81.8 26.1 %all-gather.5 = bf16[8,64,7]{1,2,0:T(8,128)(2,1)S(1)} all-gather(bf16[1,64,7]{1,2,0:T(8,128)(2,1)} %bitcast.376), channel_id=1, replica_groups=mesh['dp'=8,'mem'=4] {'dp'}, dimensions={0}, use_global_device_ids=true | all-gather | bytes 8064 | tf_op jit(solution)/shard_map/all_gather | solution.py:217
  114.1 31.2 %all_gather.122 = bf16[512,512]{1,0:T(8,128)(2,1)S(1)} all-gather(bf16[64,512]{1,0:T(8,128)(2,1)S(1)} %all_gather.121), channel_id=1, replica_groups=mesh['dp'=8,'mem'=4] {'dp'}, dimensions={0}, use_global_device_ids=true | all-gather | bytes 589824 | tf_op jit(solution)/shard_map/all_gather | solution.py:207
  154.8 31.3 %all_gather.124 = bf16[512,512]{1,0:T(8,128)(2,1)S(1)} all-gather(bf16[64,512]{1,0:T(8,128)(2,1)S(1)} %all_gather.123), channel_id=1, replica_groups=mesh['dp'=8,'mem'=4] {'dp'}, dimensions={0}, use_global_device_ids=true | all-gather | bytes 589824 | tf_op jit(solution)/shard_map/all_gather | solution.py:208
  195.6 31.2 %all_gather.119 = bf16[512,512]{1,0:T(8,128)(2,1)S(1)} all-gather(bf16[64,512]{1,0:T(8,128)(2,1)S(1)} %all_gather.118), channel_id=1, replica_groups=mesh['dp'=8,'mem'=4] {'dp'}, dimensions={0}, use_global_device_ids=true | all-gather | bytes 589824 | tf_op jit(solution)/shard_map/all_gather | solution.py:209
  236.9 31.4 %all_gather.126 = bf16[512,512]{1,0:T(8,128)(2,1)S(1)} all-gather(bf16[64,512]{1,0:T(8,128)(2,1)S(1)} %all_gather.125), channel_id=1, replica_groups=mesh['dp'=8,'mem'=4] {'dp'}, dimensions={0}, use_global_device_ids=true | all-gather | bytes 589824 | tf_op jit(solution)/shard_map/all_gather | solution.py:210
  284.2 31.5 %all_gather.128 = bf16[512,512]{1,0:T(8,128)(2,1)S(1)} all-gather(bf16[64,512]{1,0:T(8,128)(2,1)S(1)} %all_gather.127), channel_id=1, replica_groups=mesh['dp'=8,'mem'=4] {'dp'}, dimensions={0}, use_global_device_ids=true | all-gather | bytes 589824 | tf_op jit(solution)/shard_map/all_gather | solution.py:211
  324.0 31.4 %all_gather.131 = bf16[512,512]{1,0:T(8,128)(2,1)S(1)} all-gather(bf16[64,512]{1,0:T(8,128)(2,1)S(1)} %all_gather.130), channel_id=1, replica_groups=mesh['dp'=8,'mem'=4] {'dp'}, dimensions={0}, use_global_device_ids=true | all-gather | bytes 589824 | tf_op jit(solution)/shard_map/all_gather | solution.py:212
  365.4 31.5 %all_gather.135 = bf16[512,512]{1,0:T(8,128)(2,1)S(1)} all-gather(bf16[64,512]{1,0:T(8,128)(2,1)S(1)} %all_gather.134), channel_id=1, replica_groups=mesh['dp'=8,'mem'=4] {'dp'}, dimensions={0}, use_global_device_ids=true | all-gather | bytes 589824 | tf_op jit(solution)/shard_map/all_gather | solution.py:213
  445.1 33.4 %all_gather.138 = bf16[512,512]{1,0:T(8,128)(2,1)} all-gather(bf16[64,512]{1,0:T(8,128)(2,1)S(1)} %all_gather.137), channel_id=1, replica_groups=mesh['dp'=8,'mem'=4] {'dp'}, dimensions={0}, use_global_device_ids=true | all-gather | bytes 589824 | tf_op jit(solution)/shard_map/all_gather | solution.py:214
  548.4 61.2 %while.19 = (s32[]{:T(128)}, f32[16,8,256]{2,1,0:T(8,128)S(1)}, f32[16,8,256]{2,1,0:T(8,128)S(1)}, f32[16,256,512]{1,2,0:T(8,128)}, bf16[4,16,8,256]{3,2,1,0:T(8...) while((s32[]{:T(128)}, f32[16,8,256]{2,1,0:T(8,128)S(1)}, ...), condition=%wide.region_9.10_spmd, body=%wide.region_8.9_spmd.sunk | while | flops 8716293 | bytes 39518360 | solution.py:30
  636.1 20.7 %multiply_convert_fusion.3 = (bf16[4,256,2048]{2,1,0:T(8,128)(2,1)}, f32[4,256,2048]{2,1,0:T(8,128)}) fusion(f32[4,256,2048]{2,1,0:T(8,128)S(1)} %get-tuple-element.329, f32[2048]{0:T(1024)S(1)} %bitcast.332, u8[256,2048]{1,0:T(8,128)(4,1)S(1)} %get-tuple-element.261, u8[256,2048]{1,0:T(8,128)(4,1)S(1)} %get-tuple-element.260), kind=kLoop, calls=%fused_computation.28 | loop fusion | flops 148897792 | bytes 22028288 | tf_op jit(solution)/shard_map/convert_element_type | solution.py:275
  674.5 33.8 %all-gather.21.cloned.1.call-done = bf16[16,256,512]{2,1,0:T(8,128)(2,1)} async-done(((bf16[4,256,512]{2,1,0:T(8,128)(2,1)}), bf16[16,256,512]{2,1,0:T(8,128)(2,1)}) %all-gather.21.cloned.1.call-update) | async-done | bytes 4194320 | tf_op jit(solution)/shard_map/all_gather | solution.py:340
  824.8 23.6 %reduce-scatter.68.cloned.1.call-done = f32[64,512]{1,0:T(8,128)} async-done(((f32[512,512]{1,0:T(8,128)}), f32[64,512]{1,0:T(8,128)}) %reduce-scatter.68.cloned.1.call-update) | async-done | bytes 131088 | tf_op jit(solution)/shard_map/reduce_scatter | solution.py:424
  863.1 51.3 %reduce-scatter.88.cloned.1.call-done = f32[64,512]{1,0:T(8,128)} async-done(((f32[512,512]{1,0:T(8,128)}), f32[64,512]{1,0:T(8,128)}) %reduce-scatter.88.cloned.1.call-update) | async-done | bytes 131088
  916.1 64.6 %reduce-scatter.86.cloned.1.call-done = f32[64,512]{1,0:T(8,128)} async-done(((f32[512,512]{1,0:T(8,128)}), f32[64,512]{1,0:T(8,128)}) %reduce-scatter.86.cloned.1.call-update) | async-done | bytes 131088
  982.5 88.7 %reduce-scatter.74.cloned.1.call-done = f32[256,512]{1,0:T(8,128)} async-done(((f32[2048,512]{1,0:T(8,128)}), f32[256,512]{1,0:T(8,128)}) %reduce-scatter.74.cloned.1.call-update) | async-done | bytes 524304 | tf_op jit(solution)/shard_map/reduce_scatter | solution.py:426
  1073.2 89.8 %reduce-scatter.70.cloned.1.call-done = f32[64,2048]{1,0:T(8,128)} async-done(((f32[512,2048]{1,0:T(8,128)}), f32[64,2048]{1,0:T(8,128)}) %reduce-scatter.70.cloned.1.call-update) | async-done | bytes 524304 | tf_op jit(solution)/shard_map/reduce_scatter | solution.py:425
  1181.5 48.1 %reduce-scatter.62.cloned.1.call-done = f32[64,512]{1,0:T(8,128)} async-done(((f32[512,512]{1,0:T(8,128)}), f32[64,512]{1,0:T(8,128)}) %reduce-scatter.62.cloned.1.call-update) | async-done | bytes 131088 | tf_op jit(solution)/shard_map/reduce_scatter | solution.py:421
  1231.4 64.5 %reduce-scatter.56.cloned.1.call-done = f32[64,512]{1,0:T(8,128)} async-done(((f32[512,512]{1,0:T(8,128)}), f32[64,512]{1,0:T(8,128)}) %reduce-scatter.56.cloned.1.call-update) | async-done | bytes 131088 | tf_op jit(solution)/shard_map/reduce_scatter | solution.py:418
  1298.9 62.7 %reduce-scatter.54.cloned.1.call-done = f32[64,512]{1,0:T(8,128)} async-done(((f32[512,512]{1,0:T(8,128)}), f32[64,512]{1,0:T(8,128)}) %reduce-scatter.54.cloned.1.call-update) | async-done | bytes 131088 | tf_op jit(solution)/shard_map/reduce_scatter | solution.py:417
  1391.0 58.3 %reduce-scatter.60.cloned.1.call-done = f32[64,512]{1,0:T(8,128)} async-done(((f32[512,512]{1,0:T(8,128)}), f32[64,512]{1,0:T(8,128)}) %reduce-scatter.60.cloned.1.call-update) | async-done | bytes 131088 | tf_op jit(solution)/shard_map/reduce_scatter | solution.py:420
  1454.0 61.4 %reduce-scatter.58.cloned.1.call-done = f32[64,512]{1,0:T(8,128)} async-done(((f32[512,512]{1,0:T(8,128)}), f32[64,512]{1,0:T(8,128)}) %reduce-scatter.58.cloned.1.call-update) | async-done | bytes 131088 | tf_op jit(solution)/shard_map/reduce_scatter | solution.py:419
  1538.4 21.3 %reduce-scatter.64.cloned.1.call-done = bf16[64,128]{0,1:T(8,128)(2,1)} async-done(((bf16[64,512]{0,1:T(8,128)(2,1)}), bf16[64,128]{0,1:T(8,128)(2,1)}) %reduce-scatter.64.cloned.1.call-update) | async-done | bytes 16400 | tf_op jit(solution)/shard_map/reduce_scatter | solution.py:449
  1561.2 20.9 %reduce-scatter.92.cloned.1.call-done = bf16[128,256]{1,0:T(8,128)(2,1)} async-done(((bf16[512,256]{1,0:T(8,128)(2,1)}), bf16[128,256]{1,0:T(8,128)(2,1)}) %reduce-scatter.92.cloned.1.call-update) | async-done | bytes 65552
  1583.7 21.1 %reduce-scatter.72.cloned.1.call-done = bf16[64,512]{1,0:T(8,128)(2,1)} async-done(((bf16[64,2048]{1,0:T(8,128)(2,1)}), bf16[64,512]{1,0:T(8,128)(2,1)}) %reduce-scatter.72.cloned.1.call-update) | async-done | bytes 65552 | tf_op jit(solution)/shard_map/reduce_scatter | solution.py:458
  1606.3 63.1 %reduce-scatter.98.cloned.1.call-done = f32[64,3]{1,0:T(8,128)} async-done(((f32[512,3]{1,0:T(8,128)}), f32[64,3]{1,0:T(8,128)}) %reduce-scatter.98.cloned.1.call-update) | async-done | bytes 784
  1670.2 62.8 %reduce-scatter.96.cloned.1.call-done = f32[64,3]{1,0:T(8,128)} async-done(((f32[512,3]{1,0:T(8,128)}), f32[64,3]{1,0:T(8,128)}) %reduce-scatter.96.cloned.1.call-update) | async-done | bytes 784
  1733.9 62.7 %reduce-scatter.94.cloned.1.call-done = f32[64,7]{1,0:T(8,128)} async-done(((f32[512,7]{1,0:T(8,128)}), f32[64,7]{1,0:T(8,128)}) %reduce-scatter.94.cloned.1.call-update) | async-done | bytes 1808
  1797.4 62.8 %reduce-scatter.100.cloned.1.call-done = f32[64,50]{1,0:T(8,128)} async-done(((f32[512,50]{1,0:T(8,128)}), f32[64,50]{1,0:T(8,128)}) %reduce-scatter.100.cloned.1.call-update) | async-done | bytes 12816
  1926.7 20.7 %reduce-scatter.82.cloned.1.call-done = bf16[128,64]{1,0:T(8,128)(2,1)} async-done(((bf16[512,64]{1,0:T(8,128)(2,1)}), bf16[128,64]{1,0:T(8,128)(2,1)}) %reduce-scatter.82.cloned.1.call-update) | async-done | bytes 16400
  (443 shorter events, 625.5 us)
Async XLA Ops:
  7.2 349.0 %copy-start = (bf16[16,64,512]{2,1,0:T(8,128)(2,1)S(1)}, bf16[16,64,512]{2,1,0:T(8,128)(2,1)}, u32[]{:S(2)}) copy-start(bf16[16,64,512]{2,1,0:T(8,128)(2,1)} %param.25) | copy-start | bytes 3145732
  7.2 396.1 %all-gather.13.cloned.1.call-start = ((), (), s32[]{:S(2)}) async-start(), calls=%async_computation.25 | async-start | bytes 5242880 | tf_op jit(solution)/shard_map/all_gather | solution.py:258
  65.0 250.6 %copy-start.71 = (f32[1,512]{1,0:T(1,128)}, f32[1,512]{1,0:T(1,128)S(1)}, u32[]{:S(2)}) copy-start(f32[1,512]{1,0:T(1,128)S(1)} %get-tuple-element.316) | copy-start | bytes 6148
  318.2 214.1 %all-gather.15.cloned.1.call-start = ((), (), s32[]{:S(2)}) async-start(), calls=%async_computation.26 | async-start | bytes 20971520 | tf_op jit(solution)/shard_map/all_gather | solution.py:18
  424.9 201.8 %all-gather.17.cloned.1.call-start = ((), (), s32[]{:S(2)}) async-start(), calls=%async_computation.27 | async-start | bytes 2359296 | tf_op jit(solution)/shard_map/all_gather | solution.py:215
  432.0 224.8 %all-gather.19.cloned.1.call-start = ((), (), s32[]{:S(2)}) async-start(), calls=%async_computation.28 | async-start | bytes 2359296 | tf_op jit(solution)/shard_map/all_gather | solution.py:216
  438.9 269.4 %all-gather.21.cloned.1.call-start = ((), (), s32[]{:S(2)}) async-start(), calls=%async_computation.29 | async-start | bytes 5242880 | tf_op jit(solution)/shard_map/all_gather | solution.py:340
  674.5 112.9 %reduce-scatter.52.cloned.1.call-start = ((), (), s32[]{:S(2)}) async-start(), calls=%async_computation.30 | async-start | bytes 5242880 | tf_op jit(solution)/shard_map/reduce_scatter | solution.py:357
  736.5 112.0 %reduce-scatter.68.cloned.1.call-start = ((), (), s32[]{:S(2)}) async-start(), calls=%async_computation.38 | async-start | bytes 1179648 | tf_op jit(solution)/shard_map/reduce_scatter | solution.py:424
  740.6 173.8 %reduce-scatter.88.cloned.1.call-start = ((), (), s32[]{:S(2)}) async-start(), calls=%async_computation.48 | async-start | bytes 1179648
  762.1 218.6 %reduce-scatter.86.cloned.1.call-start = ((), (), s32[]{:S(2)}) async-start(), calls=%async_computation.47 | async-start | bytes 1179648
  772.6 298.5 %reduce-scatter.74.cloned.1.call-start = ((), (), s32[]{:S(2)}) async-start(), calls=%async_computation.41 | async-start | bytes 4718592 | tf_op jit(solution)/shard_map/reduce_scatter | solution.py:426
  779.6 383.5 %reduce-scatter.70.cloned.1.call-start = ((), (), s32[]{:S(2)}) async-start(), calls=%async_computation.39 | async-start | bytes 4718592 | tf_op jit(solution)/shard_map/reduce_scatter | solution.py:425
  786.6 443.0 %reduce-scatter.62.cloned.1.call-start = ((), (), s32[]{:S(2)}) async-start(), calls=%async_computation.35 | async-start | bytes 1179648 | tf_op jit(solution)/shard_map/reduce_scatter | solution.py:421
  801.1 494.8 %reduce-scatter.56.cloned.1.call-start = ((), (), s32[]{:S(2)}) async-start(), calls=%async_computation.32 | async-start | bytes 1179648 | tf_op jit(solution)/shard_map/reduce_scatter | solution.py:418
  817.8 543.8 %reduce-scatter.54.cloned.1.call-start = ((), (), s32[]{:S(2)}) async-start(), calls=%async_computation.31 | async-start | bytes 1179648 | tf_op jit(solution)/shard_map/reduce_scatter | solution.py:417
  824.8 564.8 %reduce-scatter.90.cloned.1.call-start = ((), (), s32[]{:S(2)}) async-start(), calls=%async_computation.49 | async-start | bytes 163840
  850.2 599.2 %reduce-scatter.60.cloned.1.call-start = ((), (), s32[]{:S(2)}) async-start(), calls=%async_computation.34 | async-start | bytes 1179648 | tf_op jit(solution)/shard_map/reduce_scatter | solution.py:420
  853.9 661.6 %reduce-scatter.58.cloned.1.call-start = ((), (), s32[]{:S(2)}) async-start(), calls=%async_computation.33 | async-start | bytes 1179648 | tf_op jit(solution)/shard_map/reduce_scatter | solution.py:419
  863.0 673.9 %reduce-scatter.66.cloned.1.call-start = ((), (), s32[]{:S(2)}) async-start(), calls=%async_computation.37 | async-start | bytes 163840 | tf_op jit(solution)/shard_map/reduce_scatter | solution.py:452
  916.1 643.6 %reduce-scatter.64.cloned.1.call-start = ((), (), s32[]{:S(2)}) async-start(), calls=%async_computation.36 | async-start | bytes 163840 | tf_op jit(solution)/shard_map/reduce_scatter | solution.py:449
  982.4 599.6 %reduce-scatter.92.cloned.1.call-start = ((), (), s32[]{:S(2)}) async-start(), calls=%async_computation.50 | async-start | bytes 327680
  1073.1 531.7 %reduce-scatter.72.cloned.1.call-start = ((), (), s32[]{:S(2)}) async-start(), calls=%async_computation.40 | async-start | bytes 327680 | tf_op jit(solution)/shard_map/reduce_scatter | solution.py:458
  1164.9 504.5 %reduce-scatter.98.cloned.1.call-start = ((), (), s32[]{:S(2)}) async-start(), calls=%async_computation.53 | async-start | bytes 294912
  1172.8 560.3 %reduce-scatter.96.cloned.1.call-start = ((), (), s32[]{:S(2)}) async-start(), calls=%async_computation.52 | async-start | bytes 294912
  1173.7 622.9 %reduce-scatter.94.cloned.1.call-start = ((), (), s32[]{:S(2)}) async-start(), calls=%async_computation.51 | async-start | bytes 294912
  1176.3 684.0 %reduce-scatter.100.cloned.1.call-start = ((), (), s32[]{:S(2)}) async-start(), calls=%async_computation.54 | async-start | bytes 294912
  1181.4 699.7 %reduce-scatter.84.cloned.1.call-start = ((), (), s32[]{:S(2)}) async-start(), calls=%async_computation.46 | async-start | bytes 163840
  1231.3 671.9 %reduce-scatter.78.cloned.1.call-start = ((), (), s32[]{:S(2)}) async-start(), calls=%async_computation.43 | async-start | bytes 163840
  1297.6 627.6 %reduce-scatter.76.cloned.1.call-start = ((), (), s32[]{:S(2)}) async-start(), calls=%async_computation.42 | async-start | bytes 163840
  1363.3 584.2 %reduce-scatter.82.cloned.1.call-start = ((), (), s32[]{:S(2)}) async-start(), calls=%async_computation.45 | async-start | bytes 163840
  1451.0 518.3 %reduce-scatter.80.cloned.1.call-start = ((), (), s32[]{:S(2)}) async-start(), calls=%async_computation.44 | async-start | bytes 163840
  (87 other events, 2362.9 us)
Sparse Core Ops, SparseCore 0:
  318.4 31.8 all-gather.12
  425.0 107.2 all-gather.14
  534.5 48.4 all-gather.16
  585.0 47.7 all-gather.18
  674.6 33.6 all-gather.20
  736.6 44.4 reduce-scatter.51
  784.9 63.5 reduce-scatter.67
  851.9 62.4 reduce-scatter.87
  918.2 62.5 reduce-scatter.85
  984.2 86.8 reduce-scatter.73
  1075.2 87.7 reduce-scatter.69
  1166.3 63.2 reduce-scatter.61
  1233.4 62.4 reduce-scatter.55
  1299.1 62.4 reduce-scatter.53
  1364.0 18.5 reduce-scatter.89
  1385.9 63.4 reduce-scatter.59
  1453.0 62.4 reduce-scatter.57
  1518.3 18.5 reduce-scatter.65
  1540.1 19.5 reduce-scatter.63
  1562.0 20.0 reduce-scatter.91
  1584.7 20.0 reduce-scatter.71
  1608.1 61.2 reduce-scatter.97
  1672.8 60.2 reduce-scatter.95
  1736.3 60.2 reduce-scatter.93
  1799.9 60.2 reduce-scatter.99
  1862.5 18.5 reduce-scatter.83
  1883.6 19.6 reduce-scatter.77
  1905.6 19.5 reduce-scatter.75
  1927.8 19.6 reduce-scatter.81
  1949.7 19.5 reduce-scatter.79
where the time goes:
time: 1990 us; the launch traced here: 1980 us
  waiting for transfers between devices  1090 us (55%)
  blocking collectives  468 us (24%)
  local copies, waits for them, and re-layouts  152 us (8%)
  matrix products  151 us (8%)
  other arithmetic  101 us (5%)
    unnamed x43, waiting for transfers between devices  480 us
    reduce_scatter x1, waiting for transfers between devices, shards(): lax.psum_scatter(grad_expand, 'dp', scatter_dimension=0, tiled=True)  89.8 us
    reduce_scatter x1, waiting for transfers between devices, shards(): lax.psum_scatter(grad_reduce, 'dp', scatter_dimension=0, tiled=True)  88.7 us
    reduce_scatter x1, waiting for transfers between devices, shards(): lax.psum_scatter(grad_key_self, 'dp', scatter_dimension=0, tiled=True)  64.5 us
    reduce_scatter x1, waiting for transfers between devices, shards(): lax.psum_scatter(grad_query_self, 'dp', scatter_dimension=0, tiled=True)  62.7 us
    reduce_scatter x1, waiting for transfers between devices, shards(): lax.psum_scatter(grad_value_self, 'dp', scatter_dimension=0, tiled=True)  61.4 us
    reduce_scatter x1, waiting for transfers between devices, shards(): lax.psum_scatter(grad_out_self, 'dp', scatter_dimension=0, tiled=True)  58.3 us
    unnamed x213, local copies, waits for them, and re-layouts  51.7 us
  transfers between devices with their start and end apart: 30, of which 25 were waited for; matrix products, arithmetic and copies ran while one was open for 15% of the time, Pallas kernels for 0%

commit v1 on v0

v1 whole, which is shorter than its diff:
```python
import functools
import math

import jax
import jax.numpy as jnp
from jax import lax
from jax.experimental import pallas as pl
from jax.experimental.pallas import tpu as pltpu
from jax.sharding import PartitionSpec as P

HEADS = 8
DH = 64
GROUP = 4
WIDE = GROUP * DH
EPSILON = 1e-05
SCALE = 1.0 / math.sqrt(DH)
BF = jnp.bfloat16
F32 = jnp.float32
VMEM_LIMIT = 60 * 2**20


def contract(left, right, left_dim, right_dim):
    return lax.dot_general(
        left, right, (((left_dim,), (right_dim,)), ((), ())), preferred_element_type=F32
    )


def mul(left, right):
    return contract(left, right, 1, 0)


def mul_nt(left, right):
    return contract(left, right, 1, 1)


def mul_tn(left, right):
    return contract(left, right, 0, 0)


def normalise(signal):
    centre = signal - jnp.mean(signal, axis=-1, keepdims=True)
    inverse = lax.rsqrt(jnp.mean(centre * centre, axis=-1, keepdims=True) + EPSILON)
    return centre * inverse, inverse


def norm_back(grad, scaled, inverse, gain):
    up = grad * gain
    return inverse * (
        up
        - jnp.mean(up, axis=-1, keepdims=True)
        - scaled * jnp.mean(up * scaled, axis=-1, keepdims=True)
    )


def col_sum(array):
    return jnp.sum(array.astype(F32), axis=0, keepdims=True)


def head_of_lane(rows):
    return lax.broadcasted_iota(jnp.int32, (rows, WIDE), 1) // DH


def stacked(block, lane_head):
    zero = jnp.zeros_like(block)
    return jnp.concatenate([jnp.where(lane_head == h, block, zero) for h in range(GROUP)], axis=0)


def unstacked(result, lane_head, rows):
    picked = result[:rows]
    for h in range(1, GROUP):
        picked = jnp.where(lane_head == h, result[h * rows : (h + 1) * rows], picked)
    return picked


def attend_pair(p, bias, q_ref, k_ref, v_ref, w_ref, mix_ref):
    rows = q_ref.shape[1]
    lane_head = head_of_lane(rows)
    for g in range(HEADS // GROUP):
        cols = slice(g * WIDE, (g + 1) * WIDE)
        scores = mul_nt(stacked(q_ref[p, :, cols], lane_head), k_ref[p, :, cols]) + bias
        top = jnp.max(scores, axis=-1, keepdims=True)
        raised = jnp.exp(scores - top)
        total = jnp.sum(raised, axis=-1, keepdims=True)
        weights = (raised * (1.0 / total)).astype(BF)
        w_ref[p, g] = weights
        mixed = mul(weights, v_ref[p, :, cols])
        mix_ref[p, :, cols] = unstacked(mixed, lane_head, rows).astype(BF)


def attend_pair_back(p, q_ref, k_ref, v_ref, w_ref, grad_ref, gq_ref, gk_ref, gv_ref):
    rows = q_ref.shape[1]
    lane_head = head_of_lane(rows)
    for g in range(HEADS // GROUP):
        cols = slice(g * WIDE, (g + 1) * WIDE)
        grads = stacked(grad_ref[p, :, cols], lane_head)
        weights = w_ref[p, g]
        grad_w = mul_nt(grads, v_ref[p, :, cols])
        wide = weights.astype(F32)
        offset = jnp.sum(grad_w * wide, axis=-1, keepdims=True)
        grad_s = (wide * (grad_w - offset)).astype(BF)
        grad_q = unstacked(mul(grad_s, k_ref[p, :, cols]), lane_head, rows)
        gq_ref[p, :, cols] = (grad_q * SCALE).astype(BF)
        gk_ref[p, :, cols] = mul_tn(grad_s, stacked(q_ref[p, :, cols], lane_head)).astype(BF)
        gv_ref[p, :, cols] = mul_tn(weights, grads).astype(BF)


def flat(ref):
    value = ref[...]
    return value.reshape(value.shape[0] * value.shape[1], value.shape[2])


def self_forward_kernel(
    meta, target, table, vecs, wq, wk, wv, wo, in_a, q, k, v, w, mix, after, embedded
):
    pairs, length, width = target.shape
    for p in range(pairs):
        emb = target[p].astype(F32) + table[pl.ds(meta[pairs + p], 1), :]
        embedded[p] = emb
        scaled, unused = normalise(emb)
        in_a[p] = (scaled * vecs[7:8] + vecs[10:11]).astype(BF)
    x = flat(in_a)
    shape = target.shape
    q[...] = ((mul(x, wq[...]) + vecs[0:1]).astype(BF) * SCALE).reshape(shape)
    k[...] = mul(x, wk[...]).astype(BF).reshape(shape)
    v[...] = (mul(x, wv[...]) + vecs[1:2]).astype(BF).reshape(shape)

    def pair(p, carry):
        spot = lax.broadcasted_iota(jnp.int32, (1, length), 1)
        bias = jnp.where(spot < meta[p], 0.0, -1e30)
        attend_pair(p, bias, q, k, v, w, mix)
        return carry

    lax.fori_loop(0, pairs, pair, 0)
    after[...] = embedded[...] + (mul(flat(mix), wo[...]) + vecs[2:3]).reshape(shape)


def cross_forward_kernel(
    meta, after_self, memory, vecs, wq, wk, wv, wo, in_b, q, k, v, w, mix, after
):
    pairs, length, width = after_self.shape
    shape = after_self.shape
    source = memory.shape[1]
    scaled, unused = normalise(flat(after_self))
    x = (scaled * vecs[8:9] + vecs[11:12]).astype(BF)
    in_b[...] = x.reshape(shape)
    q[...] = ((mul(x, wq[...]) + vecs[3:4]).astype(BF) * SCALE).reshape(shape)
    m = flat(memory)
    k[...] = mul(m, wk[...]).astype(BF).reshape(memory.shape)
    v[...] = (mul(m, wv[...]) + vecs[4:5]).astype(BF).reshape(memory.shape)

    def pair(p, carry):
        spot = lax.broadcasted_iota(jnp.int32, (1, source), 1)
        begin = meta[2 * pairs + p]
        end = begin + meta[3 * pairs + p]
        bias = jnp.where((spot >= begin) & (spot < end), 0.0, -1e30)
        attend_pair(p, bias, q, k, v, w, mix)
        return carry

    lax.fori_loop(0, pairs, pair, 0)
    after[...] = after_self[...] + (mul(flat(mix), wo[...]) + vecs[5:6]).reshape(shape)


def gelu_parts(value):
    size = jnp.abs(value) * math.sqrt(0.5)
    t = 1.0 / (1.0 + 0.3275911 * size)
    bell = jnp.exp(-0.5 * value * value)
    tail = (
        t
        * (
            0.5 * 0.254829592
            + t
            * (
                0.5 * -0.284496736
                + t * (0.5 * 1.421413741 + t * (0.5 * -1.453152027 + t * (0.5 * 1.061405429)))
            )
        )
        * bell
    )
    below = jnp.where(value < 0, tail, 1.0 - tail)
    slope = below + value * bell * (1.0 / math.sqrt(2.0 * math.pi))
    return value * below, slope


def feed_kernel(
    after_cross, cot, vecs, feed_bias, wi, wo, layer_out, gres, dwi, dwo, sums, dbias, x_c, out_acc, in_acc
):
    shape = after_cross.shape
    signal = flat(after_cross)
    scaled, inverse = normalise(signal)
    x_c[...] = (scaled * vecs[9:10] + vecs[12:13]).astype(BF)
    hidden = wi.shape[1]
    block = 512
    for j in range(hidden // block):
        cols = slice(j * block, (j + 1) * block)
        c = flat(cot)
        x = x_c[...]
        pre = mul(x, wi[:, cols]) + feed_bias[:, cols]
        value, slope = gelu_parts(pre)
        act = value.astype(BF)
        grad_pre = (mul_nt(c, wo[cols, :]) * slope).astype(BF)
        out_part = mul(act, wo[cols, :])
        in_part = mul_nt(grad_pre, wi[:, cols])
        if j == 0:
            out_acc[...] = out_part
            in_acc[...] = in_part
        else:
            out_acc[...] += out_part
            in_acc[...] += in_part
        dwo[cols, :] = mul_tn(act, c).astype(BF)
        dwi[:, cols] = mul_tn(x, grad_pre).astype(BF)
        dbias[:, cols] = col_sum(grad_pre)
    layer_out[...] = (signal + out_acc[...] + vecs[6:7]).astype(BF).reshape(shape)
    grad = in_acc[...]
    wide_cot = flat(cot).astype(F32)
    sums[0:1] = col_sum(wide_cot)
    sums[1:2] = col_sum(grad * scaled)
    sums[2:3] = col_sum(grad)
    gres[...] = (wide_cot + norm_back(grad, scaled, inverse, vecs[9:10])).reshape(shape)


def cross_back_kernel(
    gres, after_self, in_b, q, k, v, w, mix, memory, vecs, wq, wk, wv, wo,
    gres_out, gmem, dwq, dwk, dwv, dwo, sums, gmix, gq, gk, gv,
):
    shape = gres.shape
    pairs = shape[0]
    grad = flat(gres).astype(BF)
    sums[0:1] = col_sum(grad)
    dwo[...] = mul_tn(flat(mix), grad).astype(BF)
    gmix[...] = mul_nt(grad, wo[...]).astype(BF).reshape(shape)

    def pair(p, carry):
        attend_pair_back(p, q, k, v, w, gmix, gq, gk, gv)
        return carry

    lax.fori_loop(0, pairs, pair, 0)
    gq_f, gk_f, gv_f, m = flat(gq), flat(gk), flat(gv), flat(memory)
    sums[1:2] = col_sum(gq_f)
    sums[2:3] = col_sum(gv_f)
    dwq[...] = mul_tn(flat(in_b), gq_f).astype(BF)
    dwk[...] = mul_tn(m, gk_f).astype(BF)
    dwv[...] = mul_tn(m, gv_f).astype(BF)
    gmem[...] = (mul_nt(gk_f, wk[...]) + mul_nt(gv_f, wv[...])).astype(BF).reshape(memory.shape)
    grad_in = mul_nt(gq_f, wq[...])
    scaled, inverse = normalise(flat(after_self))
    sums[3:4] = col_sum(grad_in * scaled)
    sums[4:5] = col_sum(grad_in)
    gres_out[...] = gres[...] + norm_back(grad_in, scaled, inverse, vecs[8:9]).reshape(shape)


def self_back_kernel(
    meta, gres, target, table, in_a, q, k, v, w, mix, vecs, wq, wk, wv, wo,
    gtarget, dwq, dwk, dwv, dwo, sums, gtable, gmix, gq, gk, gv,
):
    shape = gres.shape
    pairs = shape[0]
    grad = flat(gres).astype(BF)
    sums[0:1] = col_sum(grad)
    dwo[...] = mul_tn(flat(mix), grad).astype(BF)
    gmix[...] = mul_nt(grad, wo[...]).astype(BF).reshape(shape)

    def pair(p, carry):
        attend_pair_back(p, q, k, v, w, gmix, gq, gk, gv)
        return carry

    lax.fori_loop(0, pairs, pair, 0)
    gq_f, gk_f, gv_f, x = flat(gq), flat(gk), flat(gv), flat(in_a)
    sums[1:2] = col_sum(gq_f)
    sums[2:3] = col_sum(gv_f)
    dwq[...] = mul_tn(x, gq_f).astype(BF)
    dwk[...] = mul_tn(x, gk_f).astype(BF)
    dwv[...] = mul_tn(x, gv_f).astype(BF)
    grad_in = (mul_nt(gq_f, wq[...]) + mul_nt(gk_f, wk[...]) + mul_nt(gv_f, wv[...])).reshape(shape)
    gtable[...] = jnp.zeros_like(gtable)
    for p in range(pairs):
        row = pl.ds(meta[pairs + p], 1)
        emb = target[p].astype(F32) + table[row, :]
        scaled, inverse = normalise(emb)
        gain_part = col_sum(grad_in[p] * scaled)
        shift_part = col_sum(grad_in[p])
        if p == 0:
            sums[3:4] = gain_part
            sums[4:5] = shift_part
        else:
            sums[3:4] += gain_part
            sums[4:5] += shift_part
        out = gres[p] + norm_back(grad_in[p], scaled, inverse, vecs[7:8])
        gtarget[p] = out
        gtable[row, :] += col_sum(out)


def call(kernel, outs, scratch, args, smem=0, name=None):
    space = lambda i: pltpu.SMEM if i < smem else pltpu.VMEM
    return pl.pallas_call(
        kernel,
        out_shape=[jax.ShapeDtypeStruct(s, d) for s, d in outs],
        in_specs=[pl.BlockSpec(memory_space=space(i)) for i in range(len(args))],
        out_specs=[pl.BlockSpec(memory_space=pltpu.VMEM)] * len(outs),
        scratch_shapes=[pltpu.VMEM(s, d) for s, d in scratch],
        compiler_params=pltpu.CompilerParams(vmem_limit_bytes=VMEM_LIMIT),
        name=name,
    )(*args)


def self_forward(meta, target, table, vecs, weights):
    shape = target.shape
    pairs, length, width = shape
    w_shape = (pairs, HEADS // GROUP, GROUP * length, length)
    return call(
        self_forward_kernel,
        [(shape, BF)] * 4 + [(w_shape, BF), (shape, BF), (shape, F32)],
        [(shape, F32)],
        [meta, target, table, vecs, *weights],
        1,
        "self_forward",
    )


def cross_forward(meta, after_self, memory, vecs, weights):
    shape = after_self.shape
    pairs, length, width = shape
    w_shape = (pairs, HEADS // GROUP, GROUP * length, memory.shape[1])
    return call(
        cross_forward_kernel,
        [(shape, BF)] * 2 + [(memory.shape, BF)] * 2 + [(w_shape, BF), (shape, BF), (shape, F32)],
        [],
        [meta, after_self, memory, vecs, *weights],
        1,
        "cross_forward",
    )


def feed(after_cross, cot, vecs, feed_bias, wi, wo):
    shape = after_cross.shape
    tokens = shape[0] * shape[1]
    width, hidden = wi.shape
    return call(
        feed_kernel,
        [(shape, BF), (shape, F32), (wi.shape, BF), (wo.shape, BF), ((3, width), F32), ((1, hidden), F32)],
        [((tokens, width), BF), ((tokens, width), F32), ((tokens, width), F32)],
        [after_cross, cot, vecs, feed_bias, wi, wo],
        0,
        "feed",
    )


def cross_back(gres, after_self, kept, memory, vecs, weights):
    shape = gres.shape
    mshape = memory.shape
    square = (shape[2], shape[2])
    return call(
        cross_back_kernel,
        [(shape, F32), (mshape, BF)] + [(square, BF)] * 4 + [((5, shape[2]), F32)],
        [(shape, BF), (shape, BF), (mshape, BF), (mshape, BF)],
        [gres, after_self, *kept, memory, vecs, *weights],
        0,
        "cross_back",
    )


def self_back(meta, gres, target, table, kept, vecs, weights):
    shape = gres.shape
    square = (shape[2], shape[2])
    return call(
        self_back_kernel,
        [(shape, F32)] + [(square, BF)] * 4 + [((5, shape[2]), F32), (table.shape, F32)],
        [(shape, BF)] * 4,
        [meta, gres, target, table, *kept, vecs, *weights],
        1,
        "self_back",
    )


BOTH = ("dp", "mem")


def gather_group(pieces):
    packed = jnp.concatenate([p.reshape(-1, 128) for p in pieces], axis=0)
    rows = [p.size // 128 for p in pieces]
    dp, mem = lax.axis_size("dp"), lax.axis_size("mem")
    every = lax.all_gather(packed, BOTH).reshape(dp, mem, *packed.shape)
    out, at = [], 0
    for piece, count in zip(pieces, rows):
        part = every[:, :, at : at + count].reshape(dp, mem, *piece.shape)
        at += count
        out.append(
            part.transpose(0, 2, 1, 3).reshape(dp * piece.shape[0], mem * piece.shape[1])
        )
    return out


def scatter_group(grads):
    dp, mem = lax.axis_size("dp"), lax.axis_size("mem")
    parts = []
    for g in grads:
        r, c = g.shape[0] // dp, g.shape[1] // mem
        parts.append(
            g.reshape(dp, r, mem, c).transpose(0, 2, 1, 3).reshape(dp * mem, r * c // 128, 128)
        )
    total = lax.psum_scatter(jnp.concatenate(parts, axis=1), BOTH, scatter_dimension=0)
    out, at = [], 0
    for g, part in zip(grads, parts):
        r, c = g.shape[0] // dp, g.shape[1] // mem
        count = part.shape[1]
        out.append(total[at : at + count].reshape(r, c).astype(F32))
        at += count
    return out


def shards(
    target, memory, time_steps, target_len, source_len, source_off, cotangent,
    self_query, self_key, self_value, self_out, cross_query, cross_key, cross_value, cross_out,
    feed_in, feed_out, biases, feed_bias, norm_gain, norm_shift, step_table,
):
    pairs = target.shape[0]
    width = target.shape[2]
    first = lax.axis_index("mem") * pairs
    meta = jnp.concatenate(
        [
            target_len,
            time_steps,
            lax.dynamic_slice_in_dim(source_off, first, pairs),
            lax.dynamic_slice_in_dim(source_len, first, pairs),
        ]
    )
    small = jnp.concatenate([biases, norm_gain, norm_shift, step_table], axis=0)
    small = lax.all_gather(small, "dp", axis=1, tiled=True).astype(F32)
    vecs, table = small[:13], small[13:]
    bias_row = lax.all_gather(feed_bias, "dp", axis=0, tiled=True).astype(F32)[None]
    self_w = gather_group((self_query, self_key, self_value, self_out))
    cross_w = gather_group((cross_query, cross_key, cross_value, cross_out))
    feed_w = gather_group((feed_in, feed_out))
    own_memory = lax.all_to_all(memory, "mem", 0, 1, tiled=True)

    in_a, q_a, k_a, v_a, w_a, mix_a, after_self = self_forward(meta, target, table, vecs, self_w)
    in_b, q_b, k_b, v_b, w_b, mix_b, after_cross = cross_forward(
        meta, after_self, own_memory, vecs, cross_w
    )
    layer_out, gres_c, d_in, d_out, sums_c, d_fbias = feed(
        after_cross, cotangent, vecs, bias_row, *feed_w
    )
    g_feed = scatter_group((d_in, d_out))
    gres_b, gmem, dq_b, dk_b, dv_b, do_b, sums_b = cross_back(
        gres_c, after_self, (in_b, q_b, k_b, v_b, w_b, mix_b), own_memory, vecs, cross_w
    )
    grad_memory = lax.all_to_all(gmem, "mem", 1, 0, tiled=True).astype(F32)
    g_cross = scatter_group((dq_b, dk_b, dv_b, do_b))
    grad_target, dq_a, dk_a, dv_a, do_a, sums_a, gtable = self_back(
        meta, gres_b, target, table, (in_a, q_a, k_a, v_a, w_a, mix_a), vecs, self_w
    )
    g_self = scatter_group((dq_a, dk_a, dv_a, do_a))
    small_grads = jnp.concatenate(
        [
            sums_a[1:2], sums_a[2:3], sums_a[0:1],
            sums_b[1:2], sums_b[2:3], sums_b[0:1],
            sums_c[0:1],
            sums_a[3:4], sums_b[3:4], sums_c[1:2],
            sums_a[4:5], sums_b[4:5], sums_c[2:3],
            gtable,
        ],
        axis=0,
    )
    small_grads = lax.psum(
        lax.psum_scatter(small_grads, "dp", scatter_dimension=1, tiled=True), "mem"
    )
    g_fbias = lax.psum(lax.psum_scatter(d_fbias[0], "dp", scatter_dimension=0, tiled=True), "mem")
    return (
        layer_out, grad_target, grad_memory, *g_self, *g_cross, *g_feed,
        small_grads[:7], g_fbias, small_grads[7:10], small_grads[10:13], small_grads[13:],
    )


def solution(mesh):
    rows = P(BOTH, None, None)
    piece = P("dp", "mem")
    vector = P(None, "dp")
    mem_rows = P("dp", "mem", None)
    return jax.shard_map(
        shards,
        mesh=mesh,
        in_specs=(rows, mem_rows, P(BOTH), P(BOTH), P("dp"), P("dp"), rows)
        + (piece,) * 10
        + (vector, P("dp"), vector, vector, vector),
        out_specs=(rows, rows, mem_rows) + (piece,) * 10 + (vector, P("dp"), vector, vector, vector),
        check_vma=False,
    )
```

time: 1990 us -> 764 us (0.38)
  waiting for transfers between devices: 1090 us -> 479 us
  blocking collectives: 468 us -> 83.6 us
  matrix products: 151 us -> 0 us
  Pallas kernels: 0 us -> 92.6 us
  local copies, waits for them, and re-layouts: 152 us -> 61.5 us
  other arithmetic: 101 us -> 15.8 us
    unnamed x43 -> x8, waiting for transfers between devices: 480 us -> 8.13 us
    all_gather x25 -> x2, blocking collectives: 437 us -> 52.3 us  [the longest x1 31.9 us: shards(): small = lax.all_gather(small, 'dp', axis=1, tiled=True).astype(F32)]
    reduce_scatter x12 -> x3, waiting for transfers between devices: 556 us -> 392 us  [scatter_group(): lax.psum_scatter(jnp.concatenate(parts, axis=1), BOTH, scatter_dimension=0)]
    dot_general x43 -> x0, matrix products: 150 us -> none  [the longest x10 36.1 us: outer_sum(): lax.dot_general(left_flat, right_flat, (((0,), (0,)), ((), ())), preferre...]
    pallas_call x0 -> x5, Pallas kernels: none -> 92.6 us  [call(): pl.pallas_call(kernel, out_shape=[jax.ShapeDtypeStruct(s, d) for s, d in...]
    convert_element_type x27 -> x4, other arithmetic: 46.9 us -> 4.68 us  [the longest x3 4.38 us: scatter_group(): out.append(total[at:at + count].reshape(r, c).astype(F32))]
    unnamed x213 -> x71, local copies, waits for them, and re-layouts: 51.7 us -> 16.5 us
    dynamic_slice x7 -> x2, local copies, waits for them, and re-layouts: 34.3 us -> 0.15 us  [the longest x1 0.08 us: shards(): lax.dynamic_slice_in_dim(source_off, first, pairs)]
  transfers between devices with their start and end apart: 30 -> 9, of which waited for: 25 -> 6; matrix products, arithmetic and copies ran while one was open for 15% -> 7% of each run, Pallas kernels for 0% -> 4%
where the time goes in v1:
time: 764 us; the launch traced here: 757 us
  waiting for transfers between devices  479 us (63%)
  Pallas kernels  92.6 us (12%)
  blocking collectives  83.6 us (11%)
  local copies, waits for them, and re-layouts  61.5 us (8%)
  other arithmetic  15.8 us (2%)
  between operations  15.8 us (2%)
  starting transfers between devices  8.37 us (1%)
    reduce_scatter x3, waiting for transfers between devices, scatter_group(): lax.psum_scatter(jnp.concatenate(parts, axis=1), BOTH, scatter_dimension=0)  392 us
    pallas_call x5, Pallas kernels, call(): pl.pallas_call(kernel, out_shape=[jax.ShapeDtypeStruct(s, d) for s, d in...  92.6 us
    all_gather x3, waiting for transfers between devices, gather_group(): every = lax.all_gather(packed, BOTH).reshape(dp, mem, *packed.shape)  79.4 us
    all_gather x1, blocking collectives, shards(): small = lax.all_gather(small, 'dp', axis=1, tiled=True).astype(F32)  31.9 us
    all_gather x1, blocking collectives, shards(): lax.all_gather(feed_bias, 'dp', axis=0, tiled=True).astype(F32)[None]  20.4 us
    unnamed x1, blocking collectives  20.2 us
    unnamed x71, local copies, waits for them, and re-layouts  16.5 us
  transfers between devices with their start and end apart: 9, of which 6 were waited for; matrix products, arithmetic and copies ran while one was open for 7% of the time, Pallas kernels for 4%

profile of v1, /device:TPU:0, one launch (start us, length us, event | category | flops | bytes accessed | tf_op | source)
XLA Modules:
  0.0 757.1 jit_solution(8337389110175989905)
XLA Ops:
  12.7 4.4 all-to-all-start
  17.6 31.9 %all_gather.24 = bf16[63,512]{0,1:T(8,128)(2,1)S(1)} all-gather(bf16[63,64]{0,1:T(8,128)(2,1)S(1)} %pad_maximum_fusion.6), channel_id=1, replica_groups=mesh['dp'=8,'mem'=4] {'dp'}, dimensions={1}, use_global_device_ids=true | all-gather | bytes 72576 | tf_op jit(solution)/shard_map/all_gather | solution.py:427
  51.4 20.4 %all-gather.3 = bf16[8,1,256]{2,1,0:T(2,128)(2,1)S(1)} all-gather(bf16[1,1,256]{2,1,0:T(2,128)(2,1)S(1)} %reshape.231), channel_id=1, replica_groups=mesh['dp'=8,'mem'=4] {'dp'}, dimensions={0}, use_global_device_ids=true | all-gather | bytes 4608 | tf_op jit(solution)/shard_map/all_gather | solution.py:429
  74.1 1.7 fusion.10
  78.3 51.1 %all-gather.10.cloned.1.call-done = bf16[8192,128]{1,0:T(8,128)(2,1)} async-done(((bf16[256,128]{1,0:T(8,128)(2,1)}), bf16[8192,128]{1,0:T(8,128)(2,1)}) %all-gather.10.cloned.1.call-update) | async-done | bytes 2097168 | tf_op jit(solution)/shard_map/all_gather | solution.py:381
  129.4 1.7 fusion.9
  135.1 13.9 %self_forward.1 = (bf16[4,256,512]{2,1,0:T(8,128)(2,1)}, bf16[4,256,512]{2,1,0:T(8,128)(2,1)}, bf16[4,256,512]{2,1,0:T(8,128)(2,1)}, bf16[4,256,512]{2,1,0:T(8,1...) custom-call(s32[16]{0:T(128)} %pad_add_fusion.meta, ...), custom_call_target="tpu_custom_call" | custom-call | tf_op jit(solution)/shard_map/self_forward/pallas_call | solution.py:294
  151.3 14.2 %cross_forward.1 = (bf16[4,256,512]{2,1,0:T(8,128)(2,1)}, bf16[4,256,512]{2,1,0:T(8,128)(2,1)}, bf16[4,256,512]{2,1,0:T(8,128)(2,1)}, bf16[4,256,512]{2,1,0:T(8,...) custom-call(s32[16]{0:T(128)} %pad_add_fusion.meta, ...), custom_call_target="tpu_custom_call" | custom-call | tf_op jit(solution)/shard_map/cross_forward/pallas_call | solution.py:294
  165.5 28.3 %all-gather.12.cloned.1.call-done = bf16[16384,128]{1,0:T(8,128)(2,1)} async-done(((bf16[512,128]{1,0:T(8,128)(2,1)}), bf16[16384,128]{1,0:T(8,128)(2,1)}) %all-gather.12.cloned.1.call-update) | async-done | bytes 4194320 | tf_op jit(solution)/shard_map/all_gather | solution.py:381
  193.8 4.7 slice_bitcast_fusion
  198.5 3.5 reshape.189
  202.0 1.6 copy.97
  203.6 2.0 copy.129
  205.6 1.6 copy.98
  207.2 1.7 copy.140
  208.9 25.7 %feed.1 = (bf16[4,256,512]{2,1,0:T(8,128)(2,1)}, f32[4,256,512]{2,1,0:T(8,128)}, bf16[512,2048]{1,0:T(8,128)(2,1)}, bf16[2048,512]{1,0:T(8,128)(2,1)}, f32[3,512]{1,0:T(4,128)}, /*index=5*/f32[1,2048]{1,0:T(1,128)}) custom-call(f32[4,256,512]{2,1,0:T(8,128)} %get-tuple-element.53.after_cross, bf16[4,256,512]{2,1,0:T(8,128)(2,1)} %cot.1, ...), custom_call_target="tpu_custom_call" | custom-call | tf_op jit(solution)/shard_map/feed/pallas_call | solution.py:294
  234.6 19.7 %cross_back.1 = (f32[4,256,512]{2,1,0:T(8,128)}, bf16[4,256,512]{2,1,0:T(8,128)(2,1)}, bf16[512,512]{1,0:T(8,128)(2,1)}, bf16[512,512]{1,0:T(8,128)(2,1)}, bf16[...) custom-call(f32[4,256,512]{2,1,0:T(8,128)} %get-tuple-element.55.gres, ...), custom_call_target="tpu_custom_call" | custom-call | tf_op jit(solution)/shard_map/cross_back/pallas_call | solution.py:294
  254.3 19.0 %self_back.1 = (f32[4,256,512]{2,1,0:T(8,128)}, bf16[512,512]{1,0:T(8,128)(2,1)}, bf16[512,512]{1,0:T(8,128)(2,1)}, bf16[512,512]{1,0:T(8,128)(2,1)}, bf16[512,5...) custom-call(s32[16]{0:T(128)} %pad_add_fusion.meta, f32[4,256,512]{2,1,0:T(8,128)} %get-tuple-element.62.gres, ...), custom_call_target="tpu_custom_call" | custom-call | tf_op jit(solution)/shard_map/self_back/pallas_call | solution.py:294
  284.7 3.3 reshape.208
  288.0 1.8 copy.109
  289.9 4.3 reshape.209
  294.2 2.6 reshape.210
  298.4 2.4 pad_maximum_fusion
  302.0 1.8 copy.99
  303.8 3.5 all-to-all-start.1
  308.6 20.2 %all-reduce = f32[2048]{0:T(1024)S(1)} all-reduce(f32[2048]{0:T(1024)S(1)} %bitcast.180), channel_id=9, replica_groups=mesh['dp'=8,'mem'=4] {'dp'}, use_global_device_ids=true, to_apply=%region_5.0.clone | all-reduce | flops 2048 | bytes 16384
  328.9 8.0 %reduce-scatter.13.cloned.1.call-done = f32[64,63]{1,0:T(8,128)} async-done(((f32[512,63]{1,0:T(8,128)}), f32[64,63]{1,0:T(8,128)}) %reduce-scatter.13.cloned.1.call-update) | async-done | bytes 16144
  337.7 11.1 %all-reduce.1 = (f32[63,64]{1,0:T(8,128)S(1)}, f32[256]{0:T(256)}) all-reduce(f32[63,64]{1,0:T(8,128)S(1)} %copy.112, f32[256]{0:T(256)S(1)} %dynamic-slice.1), channel_id=1, replica_groups=mesh['dp'=8,'mem'=4] {'mem'}, use_global_device_ids=true, to_apply=%region_4.0 | all-reduce | flops 4288 | bytes 34304 | tf_op jit(solution)/shard_map/psum | solution.py:463
  350.9 2.0 copy.100
  352.9 121.5 %reduce-scatter.9.cloned.1.call-done = bf16[1,256,128]{2,1,0:T(8,128)(2,1)} async-done(((bf16[32,256,128]{2,1,0:T(8,128)(2,1)}), bf16[1,256,128]{2,1,0:T(8,128)(2,1)}) %reduce-scatter.9.cloned.1.call-update) | async-done | bytes 65552 | tf_op jit(solution)/shard_map/reduce_scatter | solution.py:400
  475.8 133.1 %reduce-scatter.7.cloned.1.call-done = bf16[1,256,128]{2,1,0:T(8,128)(2,1)} async-done(((bf16[32,256,128]{2,1,0:T(8,128)(2,1)}), bf16[1,256,128]{2,1,0:T(8,128)(2,1)}) %reduce-scatter.7.cloned.1.call-update) | async-done | bytes 65552 | tf_op jit(solution)/shard_map/reduce_scatter | solution.py:400
  610.3 137.4 %reduce-scatter.11.cloned.1.call-done = bf16[1,512,128]{2,1,0:T(8,128)(2,1)} async-done(((bf16[32,512,128]{2,1,0:T(8,128)(2,1)}), bf16[1,512,128]{2,1,0:T(8,128)(2,1)}) %reduce-scatter.11.cloned.1.call-update) | async-done | bytes 131088 | tf_op jit(solution)/shard_map/reduce_scatter | solution.py:400
  (135 shorter events, 41.3 us)
Async XLA Ops:
  7.2 9.9 %copy-start.16 = (bf16[7,64]{1,0:T(8,128)(2,1)S(1)}, bf16[7,64]{1,0:T(8,128)(2,1)}, u32[]{:S(2)}) copy-start(bf16[7,64]{1,0:T(8,128)(2,1)} %param.39) | copy-start | bytes 2692
  7.2 10.0 %copy-start.17 = (bf16[3,64]{1,0:T(4,128)(2,1)S(1)}, bf16[3,64]{1,0:T(4,128)(2,1)}, u32[]{:S(2)}) copy-start(bf16[3,64]{1,0:T(4,128)(2,1)} %param.41) | copy-start | bytes 1156
  7.2 10.1 %copy-start.18 = (bf16[3,64]{1,0:T(4,128)(2,1)S(1)}, bf16[3,64]{1,0:T(4,128)(2,1)}, u32[]{:S(2)}) copy-start(bf16[3,64]{1,0:T(4,128)(2,1)} %param.42) | copy-start | bytes 1156
  7.2 10.2 %copy-start.12 = (bf16[50,64]{1,0:T(8,128)(2,1)S(1)}, bf16[50,64]{1,0:T(8,128)(2,1)}, u32[]{:S(2)}) copy-start(bf16[50,64]{1,0:T(8,128)(2,1)} %param.43) | copy-start | bytes 19204
  7.2 66.9 %all-gather.8.cloned.1.call-start = ((), (), s32[]{:S(2)}) async-start(), calls=%async_computation.9 | async-start | bytes 2162688 | tf_op jit(solution)/shard_map/all_gather | solution.py:381
  8.7 41.0 %copy-start.21 = (s32[16]{0:T(128)S(1)}, s32[16]{0:T(128)}, u32[]{:S(2)}) copy-start(s32[16]{0:T(128)} %param.27) | copy-start | bytes 196
  8.7 41.1 %copy-start.22 = (s32[16]{0:T(128)S(1)}, s32[16]{0:T(128)}, u32[]{:S(2)}) copy-start(s32[16]{0:T(128)} %param.26) | copy-start | bytes 196
  8.7 120.7 %all-gather.10.cloned.1.call-start = ((), (), s32[]{:S(2)}) async-start(), calls=%async_computation.10 | async-start | bytes 2162688 | tf_op jit(solution)/shard_map/all_gather | solution.py:381
  10.2 183.6 %all-gather.12.cloned.1.call-start = ((), (), s32[]{:S(2)}) async-start(), calls=%async_computation.11 | async-start | bytes 4325376 | tf_op jit(solution)/shard_map/all_gather | solution.py:381
  12.7 38.7 %copy-start.23 = (bf16[256]{0:T(256)(128)(2,1)S(1)}, bf16[256]{0:T(256)(128)(2,1)}, u32[]{:S(2)}) copy-start(bf16[256]{0:T(256)(128)(2,1)} %param.40) | copy-start | bytes 1540
  12.7 59.7 %copy-start.19 = (s32[4]{0:T(128)S(1)}, s32[4]{0:T(128)}, u32[]{:S(2)}) copy-start(s32[4]{0:T(128)} %param.24) | copy-start | bytes 52
  12.7 59.7 %copy-start.20 = (s32[4]{0:T(128)S(1)}, s32[4]{0:T(128)}, u32[]{:S(2)}) copy-start(s32[4]{0:T(128)} %param.25) | copy-start | bytes 52
  12.7 60.2 %all-to-all-start = ((bf16[16,64,512]{2,1,0:T(8,128)(2,1)}), bf16[16,64,512]{2,1,0:T(8,128)(2,1)S(1)}, u32[]{:S(2)}, u32[]{:S(2)}) async-start(bf16[16,64,512]{2,1,0:T(8,128)(2,1)} %param.23), calls=%async_computation | async-start | bytes 2097152 | tf_op jit(solution)/shard_map/all_to_all | solution.py:433
  17.1 319.8 %reduce-scatter.13.cloned.1.call-start = ((), (), s32[]{:S(2)}) async-start(), calls=%async_computation.12 | async-start | bytes 294912
  132.0 2.0 copy-start.2
  203.6 2.0 copy-start
  254.3 20.6 %copy-start.14 = (f32[5,512]{1,0:T(8,128)S(1)}, f32[5,512]{1,0:T(8,128)}, u32[]{:S(2)}) copy-start(f32[5,512]{1,0:T(8,128)} %get-tuple-element.82) | copy-start | bytes 30724
  254.3 20.6 %copy-start.15 = (f32[3,512]{1,0:T(4,128)S(1)}, f32[3,512]{1,0:T(4,128)}, u32[]{:S(2)}) copy-start(f32[3,512]{1,0:T(4,128)} %get-tuple-element.83) | copy-start | bytes 18436
  254.3 22.9 %copy-start.11 = (bf16[512,512]{1,0:T(8,128)(2,1)S(1)}, bf16[512,512]{1,0:T(8,128)(2,1)}, u32[]{:S(2)}) copy-start(bf16[512,512]{1,0:T(8,128)(2,1)} %get-tuple-element.75) | copy-start | bytes 1572868
  273.3 4.1 copy-start.10
  276.9 197.5 %reduce-scatter.9.cloned.1.call-start = ((), (), s32[]{:S(2)}) async-start(), calls=%async_computation.7 | async-start | bytes 2162688 | tf_op jit(solution)/shard_map/reduce_scatter | solution.py:400
  277.5 1.1 copy-start.7
  280.4 1.3 copy-start.6
  280.4 328.4 %reduce-scatter.7.cloned.1.call-start = ((), (), s32[]{:S(2)}) async-start(), calls=%async_computation.6 | async-start | bytes 2162688 | tf_op jit(solution)/shard_map/reduce_scatter | solution.py:400
  281.4 1.1 copy-start.5
  281.7 1.1 copy-start.4
  284.6 463.0 %reduce-scatter.11.cloned.1.call-start = ((), (), s32[]{:S(2)}) async-start(), calls=%async_computation.8 | async-start | bytes 4325376 | tf_op jit(solution)/shard_map/reduce_scatter | solution.py:400
  296.8 1.6 copy-start.1
  300.8 1.2 copy-start.3
  302.0 5.3 copy-start.24
  302.0 6.6 copy-start.13
  303.8 46.8 %all-to-all-start.1 = ((bf16[4,256,512]{2,0,1:T(4,128)(2,1)}), bf16[4,256,512]{2,0,1:T(4,128)(2,1)S(1)}, u32[]{:S(2)}, u32[]{:S(2)}) async-start(bf16[4,256,512]{2,0,1:T(4,128)(2,1)} %copy.99), calls=%async_computation.1 | async-start | bytes 2097152 | tf_op jit(solution)/shard_map/all_to_all | solution.py:446
  (2 other events, 2.1 us)
Sparse Core Ops, SparseCore 0:
  11.5 59.1 all-gather.7
  74.1 55.2 all-gather.9
  132.9 60.8 all-gather.11
  277.0 59.8 reduce-scatter.12
  339.0 135.3 reduce-scatter.8
  476.6 132.2 reduce-scatter.6
  611.1 136.4 reduce-scatter.10
